TPU v7x, 32 devices: a whole 2x2x4 slice. The times are simulated.
32 devices in a mesh: groups: 2 (over y), replica: 8 (over z, x), tensor: 2 (over core).
Axes of the slice: x: 2, y: 2, z: 4, core: 2. Of those that a mesh axis runs over, the one named last changes fastest.
Arguments:
- queries: bfloat16 [32, 4096], P(('groups', 'replica'), 'tensor'), parts along dimension 0
- new_keys: bfloat16 [32, 512], P(('groups', 'replica'), 'tensor'), parts along dimension 0, may hold values from -6 to 6
- new_values: bfloat16 [32, 512], P(('groups', 'replica'), 'tensor'), parts along dimension 0, may hold values from -6 to 6
- key_cache: bfloat16 [32, 1024, 512], P(('groups', 'replica'), None, 'tensor'), parts along dimension 0
- value_cache: bfloat16 [32, 1024, 512], P(('groups', 'replica'), None, 'tensor'), parts along dimension 0, may hold values from -6 to 6
- lengths: int32 [32], P(('groups', 'replica')), parts along dimension 0, may hold values from 2 to 1024, as said below
- base_held: bfloat16 [5120, 512], P('replica', 'tensor'), may hold values from -0.078125 to 0.078125
- adapter_a: bfloat16 [5120, 16], P('replica'), may hold values from -6 to 6
- adapter_b: bfloat16 [16, 512], P(None, 'tensor'), may hold values from -0.01953125 to 0.01953125
- owners: int32 [8], replicated, may hold values from 0 to 7, each once
Outputs:
- handed_rows: bfloat16 [32, 4096], P(('groups', 'replica'), 'tensor'), parts along dimension 0
- block_values: bfloat16 [10240, 512], P('groups', 'tensor'), parts along dimension 0
- block_scales: float32 [80, 4], P('groups', 'tensor'), parts along dimension 0
There are 2 independent parts, one for each index of `groups`. A program takes and returns all parts, laid end to end along the dimension named above; an argument that names none is the same for every part. Nothing has to cross between parts.
Inputs may be any that keep to these rules, and one draw needn't show every extreme that they name: Some row has lengths equal to 1024.
All inputs are finite; a program needn't handle non-finite values. Where the computation divides by a largest or mean magnitude, that divisor is 1e-20 or more.
Results may differ from a plain program's by a relative error of at most 0.0059.
Values may be sent and summed in bfloat16 or wider, within the bound.
A program may use at most 64 MiB of HBM per device.

v0:
```python
import jax
import jax.numpy as jnp
from jax import lax
from jax.sharding import PartitionSpec as P

HD = 128
BLOCK = 128


def from_behind(value, axis, steps):
    count = lax.axis_size(axis)
    pairs = [(source, (source + steps) % count) for source in range(count)]
    return lax.ppermute(value, axis, pairs)


def merge_rows(base_rows, factor_rows, adapter_b):
    return (
        base_rows.astype(jnp.float32)
        + jnp.dot(factor_rows, adapter_b, preferred_element_type=jnp.float32)
    ).astype(jnp.bfloat16)


def on_device(
    queries,
    new_keys,
    new_values,
    key_cache,
    value_cache,
    lengths,
    base_held,
    adapter_a,
    adapter_b,
    owners,
):
    replicas = lax.axis_size("replica")
    slice_rows, columns = base_held.shape
    merged = merge_rows(base_held, adapter_a, adapter_b)
    everything = lax.all_gather(merged, "replica", axis=0, tiled=True)
    assembled = jnp.take(everything.reshape(replicas, slice_rows, columns), owners, axis=0).reshape(
        replicas * slice_rows, columns
    )
    total_rows = assembled.shape[0]
    tiled = assembled.astype(jnp.float32).reshape(
        total_rows // BLOCK, BLOCK, columns // BLOCK, BLOCK
    )
    block_scales = jnp.max(jnp.abs(tiled), axis=(1, 3)) + 1e-06
    block_values = (
        (tiled / block_scales[:, None, :, None]).reshape(total_rows, columns).astype(jnp.bfloat16)
    )
    row_count = queries.shape[0]
    slot_count = key_cache.shape[1]
    kv_heads = key_cache.shape[2] // HD
    per_group = queries.shape[1] // HD // kv_heads
    scaling = 1.0 / HD**0.5
    query_heads = queries.reshape(row_count, kv_heads, per_group, HD)
    cached_keys = key_cache.reshape(row_count, slot_count, kv_heads, HD)
    cached_values = value_cache.reshape(row_count, slot_count, kv_heads, HD)
    scores = (
        jnp.einsum("rgqd,rlgd->rgql", query_heads, cached_keys, preferred_element_type=jnp.float32)
        * scaling
    )
    usable = jnp.arange(slot_count)[None, None, None, :] < lengths[:, None, None, None]
    scores = jnp.where(usable, scores, -jnp.inf)
    own_score = (
        jnp.einsum(
            "rgqd,rgd->rgq",
            query_heads,
            new_keys.reshape(row_count, kv_heads, HD),
            preferred_element_type=jnp.float32,
        )
        * scaling
    )
    highest = jnp.maximum(jnp.max(scores, axis=-1), own_score)
    raised = jnp.exp(scores - highest[..., None])
    own_raised = jnp.exp(own_score - highest)
    totals = jnp.sum(raised, axis=-1) + own_raised
    weights = (raised / totals[..., None]).astype(jnp.bfloat16)
    own_weight = (own_raised / totals).astype(jnp.bfloat16)
    mixed = jnp.einsum(
        "rgql,rlgd->rgqd", weights, cached_values, preferred_element_type=jnp.float32
    )
    mixed = mixed + own_weight.astype(jnp.float32)[..., None] * new_values.reshape(
        row_count, kv_heads, 1, HD
    ).astype(jnp.float32)
    attended = mixed.reshape(row_count, kv_heads * per_group * HD).astype(jnp.bfloat16)
    handed_rows = from_behind(attended, "replica", 1)
    return (handed_rows, block_values, block_scales)


def solution(mesh):
    in_specs = (
        P(("groups", "replica"), "tensor"),
        P(("groups", "replica"), "tensor"),
        P(("groups", "replica"), "tensor"),
        P(("groups", "replica"), None, "tensor"),
        P(("groups", "replica"), None, "tensor"),
        P(("groups", "replica")),
        P("replica", "tensor"),
        P("replica", None),
        P(None, "tensor"),
        P(),
    )
    out_specs = (P(("groups", "replica"), "tensor"), P("groups", "tensor"), P("groups", "tensor"))
    return jax.shard_map(
        on_device, mesh=mesh, in_specs=in_specs, out_specs=out_specs, check_vma=False
    )
```

profile of v0, /device:TPU:0, one launch (start us, length us, event | category | flops | bytes accessed | tf_op | source)
XLA Modules:
  0.0 96.6 jit_solution(3591475059554518748)
XLA Ops:
  7.2 0.0 copy-start
  7.2 0.0 copy-start.2
  7.2 0.0 all-gather.2.cloned.1.call-start
  7.2 2.1 %fusion.1 = bf16[640,256]{1,0:T(8,128)(2,1)} fusion(bf16[640,16]{0,1:T(8,128)(2,1)} %param.17, bf16[16,256]{1,0:T(8,128)(2,1)} %param.18, bf16[640,256]{1,0:T(8,128)(2,1)} %param.16), kind=kOutput, calls=%fused_computation.7 | convolution fusion | flops 5734400 | bytes 684032 | tf_op jit(solution)/shard_map/dot_general | solution.py:19
  9.3 0.0 all-gather.2.cloned.1.call-update
  9.4 0.7 reshape.99
  10.1 0.7 reshape.86
  10.7 0.7 iota_compare_fusion
  11.5 0.8 fusion.12
  12.3 0.0 copy-done
  12.3 1.2 %fusion.19 = (f32[2,2,8]{2,1,0:T(2,128)S(1)}, f32[2,2,8,1024]{3,2,1,0:T(8,128)S(1)}) fusion(bf16[1,2,16,128]{3,1,2,0:T(2,128)(2,1)} %bitcast.52, pred[2,1024]{1,0:T(4,128)(4,1)S(1)} %iota_compare_fusion, bf16[2,1024,256]{2,1,0:T(8,128)(2,1)S(1)} %copy-done), kind=kOutput, calls=%fused_computation.39 | convolution fusion | flops 8486880 | bytes 1190016 | tf_op jit(solution)/shard_map/rgqd,rlgd->rgql/dot_general | solution.py:59
  13.5 0.2 fusion.9
  13.7 1.5 %fusion.4 = bf16[1,2,16,128]{3,2,1,0:T(8,128)(2,1)S(1)} fusion(f32[2,2,8,1024]{3,2,1,0:T(8,128)S(1)} %get-tuple-element.9, f32[2,2,8]{2,1,0:T(2,128)S(1)} %get-tuple-element.7, f32[2,2,8]{2,1,0:T(2,128)S(1)} %multiply_maximum_fusion, f32[2,2,128]{2,1,0:T(2,128)S(1)} %reshape.86, f32[2,2,8]{2,1,0:T(2,128)S(1)} %get-tuple-element.6, ...), kind=kOutput, calls=%fused_computation.12 | convolution fusion | flops 8499200 | bytes 1190272 | tf_op jit(solution)/shard_map/rgql,rlgd->rgqd/dot_general | solution.py:79
  15.2 3.0 %collective-permute-start = (bf16[2,2048]{1,0:T(2,128)(2,1)S(1)}, bf16[2,2048]{1,0:T(2,128)(2,1)S(1)}, u32[]{:S(2)}, u32[]{:S(2)}) collective-permute-start(bf16[2,2048]{1,0:T(2,128)(2,1)S(1)} %bitcast.55), channel_id=1, source_target_pairs={{0,2},{2,4},{4,6},{6,8},{8,10},{10,12},{12,14},{14,0},{1,3},{3,5},... | collective-permute-start | bytes 24584 | tf_op jit(solution)/shard_map/ppermute | solution.py:13
  18.2 0.0 copy-done.2
  18.2 0.1 broadcast_in_dim.44
  18.3 0.1 broadcast_in_dim.45
  18.4 0.1 broadcast_bitcast_fusion
  18.5 4.4 %collective-permute-done = bf16[2,2048]{1,0:T(2,128)(2,1)S(1)} collective-permute-done((bf16[2,2048]{1,0:T(2,128)(2,1)S(1)}, bf16[2,2048]{1,0:T(2,128)(2,1)S(1)}, u32[]{:S(2)}, u32[]{:S(2)}) %collective-permute-start) | collective-permute-done | bytes 8224 | tf_op jit(solution)/shard_map/ppermute | solution.py:13
  22.9 45.3 %all-gather.2.cloned.1.call-done = bf16[5120,256]{1,0:T(8,128)(2,1)} async-done(((bf16[640,256]{1,0:T(8,128)(2,1)}), bf16[5120,256]{1,0:T(8,128)(2,1)}) %all-gather.2.cloned.1.call-update) | async-done | bytes 2621456 | tf_op jit(solution)/shard_map/all_gather | solution.py:38
  68.2 3.9 %gather_fusion = bf16[8,640,256]{2,1,0:T(8,128)(2,1)} fusion(bf16[8,640,256]{2,1,0:T(8,128)(2,1)} %bitcast.50, s32[1024]{0:T(1024)S(1)} %pad_clamp_fusion), kind=kCustom, calls=%fused_computation | custom fusion | bytes 5242912 | tf_op jit(solution)/shard_map/jit(_take)/gather | solution.py:39
  72.1 4.9 %gather.10 = bf16[40,128,2,128]{3,2,1,0:T(2,128)(2,1)} reshape(bf16[8,640,256]{2,1,0:T(8,128)(2,1)} %gather_fusion) | data formatting | bytes 5242880 | tf_op jit(solution)/shard_map/jit(_take)/gather | solution.py:39
  77.0 5.3 %abs_reduce_fusion = f32[40,2]{1,0:T(8,128)S(1)} fusion(bf16[40,128,2,128]{3,2,1,0:T(2,128)(2,1)} %gather.10, pred[40]{0:T(512)(128)(4,1)S(1)} %broadcast_in_dim.45), kind=kLoop, calls=%fused_computation.3 | loop fusion | flops 5242800 | bytes 2621800 | tf_op jit(solution)/shard_map/reduce_max | solution.py:46
  82.3 0.6 copy.18
  82.9 0.0 copy-start.1
  82.9 1.4 %div.25 = f32[40,128,2,128]{3,2,1,0:T(2,128)S(1)} broadcast(f32[40,2]{1,0:T(8,128)S(1)} %broadcast_add_fusion), dimensions={0,2} | broadcast | bytes 5243200 | tf_op jit(solution)/shard_map/div | solution.py:48
  84.4 0.3 copy-done.1
  84.7 4.4 %fusion = bf16[5120,256]{1,0:T(8,128)(2,1)} fusion(f32[640,8,2,128]{3,2,1,0:T(2,128)S(1)} %bitcast.49, bf16[8,640,256]{2,1,0:T(8,128)(2,1)S(1)} %copy-done.1, pred[5120]{0:T(1024)(128)(4,1)S(1)} %broadcast_bitcast_fusion), kind=kLoop, calls=%fused_computation.2 | loop fusion | flops 5242880 | bytes 10490880 | tf_op jit(solution)/shard_map/convert_element_type | solution.py:48
  89.1 0.6 copy.50
  (7 shorter events, 0.1 us)
Async XLA Ops:
  7.2 5.1 %copy-start = (bf16[2,1024,256]{2,1,0:T(8,128)(2,1)S(1)}, bf16[2,1024,256]{2,1,0:T(8,128)(2,1)}, u32[]{:S(2)}) copy-start(bf16[2,1024,256]{2,1,0:T(8,128)(2,1)} %param.13) | copy-start | bytes 3145732
  7.2 11.0 %copy-start.2 = (s32[8]{0:T(128)S(1)}, s32[8]{0:T(128)}, u32[]{:S(2)}) copy-start(s32[8]{0:T(128)} %param.19) | copy-start | bytes 100
  7.2 61.0 %all-gather.2.cloned.1.call-start = ((), (), s32[]{:S(2)}) async-start(), calls=%async_computation | async-start | bytes 2949120 | tf_op jit(solution)/shard_map/all_gather | solution.py:38
  15.2 7.7 %collective-permute-start = (bf16[2,2048]{1,0:T(2,128)(2,1)S(1)}, bf16[2,2048]{1,0:T(2,128)(2,1)S(1)}, u32[]{:S(2)}, u32[]{:S(2)}) collective-permute-start(bf16[2,2048]{1,0:T(2,128)(2,1)S(1)} %bitcast.55), channel_id=1, source_target_pairs={{0,2},{2,4},{4,6},{6,8},{8,10},{10,12},{12,14},{14,0},{1,3},{3,5},... | collective-permute-start | bytes 24584 | tf_op jit(solution)/shard_map/ppermute | solution.py:13
  82.9 1.7 %copy-start.1 = (bf16[8,640,256]{2,1,0:T(8,128)(2,1)S(1)}, bf16[8,640,256]{2,1,0:T(8,128)(2,1)}, u32[]{:S(2)}) copy-start(bf16[8,640,256]{2,1,0:T(8,128)(2,1)} %gather_fusion) | copy-start | bytes 7864324
Sparse Core Ops, SparseCore 0:
  10.8 57.3 all-gather.1
where the time goes:
time: 97.1 us; the launch traced here: 96.6 us
  waiting for transfers between devices  49.7 us (51%)
  between operations  14.1 us (15%)
  local copies, waits for them, and re-layouts  13.5 us (14%)
  other arithmetic  10.7 us (11%)
  matrix products  5.6 us (6%)
  starting transfers between devices  3.03 us (3%)
    all_gather x1, waiting for transfers between devices, on_device(): everything = lax.all_gather(merged, 'replica', axis=0, tiled=True)  45.3 us
    gather x2, local copies, waits for them, and re-layouts, on_device(): jnp.take(everything.reshape(replicas, slice_rows, columns), owners, axis=0)  8.84 us
    reduce_max x1, other arithmetic, on_device(): block_scales = jnp.max(jnp.abs(tiled), axis=(1, 3)) + 1e-06  5.28 us
    convert_element_type x1, other arithmetic, on_device(): (tiled / block_scales[:, None, :, None]).reshape(total_rows, columns)  4.45 us
    ppermute x1, waiting for transfers between devices, from_behind(): return lax.ppermute(value, axis, pairs)  4.39 us
    ppermute x1, starting transfers between devices, from_behind(): return lax.ppermute(value, axis, pairs)  2.99 us
    dot_general x1, matrix products, merge_rows(): jnp.dot(factor_rows, adapter_b, preferred_element_type=jnp.float32)  2.1 us
  transfers between devices with their start and end apart: 2, of which 2 were waited for; matrix products, arithmetic and copies ran while one was open for 6% of the time, Pallas kernels for 0%

commit v1 on v0

--- a/solution.py
+++ b/solution.py
@@ -1,6 +1,8 @@
 import jax
 import jax.numpy as jnp
 from jax import lax
+from jax.experimental import pallas as pl
+from jax.experimental.pallas import tpu as pltpu
 from jax.sharding import PartitionSpec as P
 
 HD = 128
@@ -87,7 +89,400 @@
     return (handed_rows, block_values, block_scales)
 
 
+def sixteen(rows):
+    return max(16, rows // 16 * 16)
+
+
+def gather_kernel(
+    queries_ref,
+    new_keys_ref,
+    new_values_ref,
+    lengths_ref,
+    base_ref,
+    factor_ref,
+    adapter_b_ref,
+    keys_hbm,
+    values_hbm,
+    gathered,
+    scales_all,
+    handed,
+    own,
+    own_scales,
+    attended,
+    keys,
+    values,
+    local_sem,
+    z_send,
+    z_recv,
+    x_send,
+    x_recv,
+    y_send,
+    y_recv,
+    scale_send,
+    scale_recv,
+    hand_sem,
+):
+    group = lax.axis_index("groups")
+    me = lax.axis_index("replica")
+    count = lax.axis_size("replica")
+    depth = count // 2
+    z = me // 2
+    x = me % 2
+    rows, columns = base_ref.shape
+    row_count, slot_count, _ = keys.shape
+    kv_heads = columns // HD
+    per_group = queries_ref.shape[1] // HD // kv_heads
+
+    keys_in = pltpu.make_async_copy(keys_hbm, keys, local_sem.at[0])
+    values_in = pltpu.make_async_copy(values_hbm, values, local_sem.at[1])
+    keys_in.start()
+    values_in.start()
+
+    barrier = pltpu.get_barrier_semaphore()
+    for step in range(1, count):
+        pl.semaphore_signal(
+            barrier, inc=1, device_id={"replica": lax.rem(me + step, count)}
+        )
+    pl.semaphore_signal(barrier, inc=1, device_id={"groups": 1 - group})
+
+    lane = lax.broadcasted_iota(jnp.int32, own_scales.shape, 1)
+    line = lax.broadcasted_iota(jnp.int32, own_scales.shape, 0)
+    blocks = rows // BLOCK
+    spread = jnp.zeros(own_scales.shape, jnp.float32)
+    for block in range(blocks):
+        part = pl.ds(block * BLOCK, BLOCK)
+        product = lax.dot_general(
+            factor_ref[:, block * BLOCK : (block + 1) * BLOCK],
+            adapter_b_ref[...],
+            (((0,), (0,)), ((), ())),
+            preferred_element_type=jnp.float32,
+        )
+        merged = (base_ref[part, :].astype(jnp.float32) + product).astype(jnp.bfloat16)
+        for column in range(columns // BLOCK):
+            tile = merged[:, column * BLOCK : (column + 1) * BLOCK].astype(jnp.float32)
+            scale = jnp.max(jnp.abs(tile), axis=(0, 1), keepdims=True) + 1e-06
+            own[part, column * BLOCK : (column + 1) * BLOCK] = (tile / scale).astype(jnp.bfloat16)
+            spread = jnp.where((lane % blocks == block) & (line == column), scale, spread)
+    own_scales[...] = spread
+
+    pl.semaphore_wait(barrier, count)
+
+    z_end, x_end = sixteen(rows * 31 // 40), sixteen(rows * 3 // 5)
+    cut = sixteen(rows * 2 // 5)
+    z_pieces = ((0, cut), (cut, z_end))
+    x_pieces = ((0, cut), (cut, x_end))
+    yx_piece, yz_piece = (0, rows - x_end), (0, rows - z_end)
+
+    def window(ref, piece, side):
+        low, high = piece
+        start = pl.multiple_of(low + side * (rows - high - low), 16)
+        return ref.at[pl.ds(start, high - low)]
+
+    def copy(source, plane, column, piece, side, send, recv, device):
+        target = gathered.at[plane * 2 + column]
+        source = target if source is None else source
+        return pltpu.make_async_remote_copy(
+            src_ref=window(source, piece, side),
+            dst_ref=window(target, piece, side),
+            send_sem=send,
+            recv_sem=recv,
+            device_id=device,
+        )
+
+    def z_copy(plane, piece, way, source=None):
+        return copy(
+            source,
+            plane,
+            x,
+            z_pieces[piece],
+            group,
+            z_send.at[(way + 1) // 2, plane, piece],
+            z_recv.at[plane, piece],
+            {"replica": lax.rem(me + 2 * way + count, count)},
+        )
+
+    def x_copy(plane, piece, column, source=None):
+        return copy(
+            source,
+            plane,
+            column,
+            x_pieces[piece],
+            group,
+            x_send.at[plane, piece],
+            x_recv.at[plane, piece],
+            {"replica": z * 2 + 1 - x},
+        )
+
+    def y_copy(plane, column, which, side):
+        return copy(
+            None,
+            plane,
+            column,
+            (yx_piece, yz_piece)[which],
+            side,
+            y_send.at[which, plane],
+            y_recv.at[which, plane],
+            {"groups": 1 - group},
+        )
+
+    def scale_copy(step):
+        return pltpu.make_async_remote_copy(
+            src_ref=own_scales,
+            dst_ref=scales_all.at[me],
+            send_sem=scale_send.at[step],
+            recv_sem=scale_recv.at[step],
+            device_id={"replica": lax.rem(me + step, count)},
+        )
+
+    def attend(row, head):
+        first = head * per_group
+        query = jnp.concatenate(
+            [
+                queries_ref[row : row + 1, (first + i) * HD : (first + i + 1) * HD].astype(
+                    jnp.float32
+                )
+                for i in range(per_group)
+            ],
+            axis=0,
+        )
+        wide = slice(head * HD, (head + 1) * HD)
+        scaling = 1.0 / HD**0.5
+        scores = (
+            lax.dot_general(
+                query.astype(jnp.bfloat16),
+                keys[row, :, wide],
+                (((1,), (1,)), ((), ())),
+                preferred_element_type=jnp.float32,
+            )
+            * scaling
+        )
+        slot = lax.broadcasted_iota(jnp.int32, scores.shape, 1)
+        scores = jnp.where(slot < lengths_ref[row], scores, -jnp.inf)
+        new_key = new_keys_ref[row : row + 1, wide].astype(jnp.float32)
+        own_score = jnp.sum(query * new_key, axis=1, keepdims=True) * scaling
+        highest = jnp.maximum(jnp.max(scores, axis=1, keepdims=True), own_score)
+        raised = jnp.exp(scores - highest)
+        own_raised = jnp.exp(own_score - highest)
+        totals = jnp.sum(raised, axis=1, keepdims=True) + own_raised
+        weights = (raised / totals).astype(jnp.bfloat16)
+        own_weight = (own_raised / totals).astype(jnp.bfloat16).astype(jnp.float32)
+        mixed = jnp.dot(weights, values[row, :, wide], preferred_element_type=jnp.float32)
+        new_value = new_values_ref[row : row + 1, wide].astype(jnp.float32)
+        return mixed + own_weight * new_value
+
+    for piece in range(2):
+
+        @pl.when(z < depth - 1)
+        def _():
+            z_copy(z, piece, 1, own).start()
+
+        @pl.when(z > 0)
+        def _():
+            z_copy(z, piece, -1, own).start()
+
+        x_copy(z, piece, x, own).start()
+    for step in range(1, count):
+        scale_copy(step).start()
+    own_out = pltpu.make_async_copy(own, gathered.at[me], local_sem.at[2])
+    own_out.start()
+    scales_out = pltpu.make_async_copy(own_scales, scales_all.at[me], local_sem.at[3])
+    scales_out.start()
+
+    def z_step(plane, piece, way):
+        z_copy(plane, piece, way).wait_recv()
+
+        @pl.when((z + way >= 0) & (z + way < depth))
+        def _():
+            z_copy(plane, piece, way).start()
+
+        x_copy(plane, piece, x).start()
+        if piece == 0:
+            y_copy(plane, x, 1, group).start()
+
+    def x_step(plane, piece):
+        x_copy(plane, piece, 1 - x).wait_recv()
+        if piece == 0:
+            y_copy(plane, 1 - x, 0, group).start()
+
+    keys_in.wait()
+    values_in.wait()
+    units = [(row, head) for row in range(row_count) for head in range(kv_heads)]
+    done = [attend(*unit) for unit in units]
+    tall = jnp.concatenate(done, axis=0)
+    attended[...] = tall.astype(jnp.bfloat16)
+    hand = pltpu.make_async_remote_copy(
+        src_ref=attended,
+        dst_ref=handed,
+        send_sem=hand_sem.at[0],
+        recv_sem=hand_sem.at[1],
+        device_id={"replica": lax.rem(me + 1, count)},
+    )
+    hand.start()
+
+    for step in range(1, depth + 1):
+        for piece in range(2):
+            if step < depth:
+
+                @pl.when(z - step >= 0)
+                def _():
+                    z_step(z - step, piece, 1)
+
+                @pl.when(z + step < depth)
+                def _():
+                    z_step(z + step, piece, -1)
+
+            if step == 1:
+                x_step(z, piece)
+            else:
+
+                @pl.when(z - step + 1 >= 0)
+                def _():
+                    x_step(z - step + 1, piece)
+
+                @pl.when(z + step - 1 < depth)
+                def _():
+                    x_step(z + step - 1, piece)
+
+    own_out.wait()
+    scales_out.wait()
+    hand.wait()
+    for step in range(1, count):
+        scale_copy(step).wait()
+    for plane in range(depth):
+        for piece in range(2):
+
+            @pl.when((plane <= z) & (z < depth - 1))
+            def _():
+                z_copy(plane, piece, 1).wait_send()
+
+            @pl.when((plane >= z) & (z > 0))
+            def _():
+                z_copy(plane, piece, -1).wait_send()
+
+            x_copy(plane, piece, x).wait_send()
+        y_copy(plane, 1 - x, 0, group).wait_send()
+        y_copy(plane, 1 - x, 0, 1 - group).wait_recv()
+
+        @pl.when(z != plane)
+        def _():
+            y_copy(plane, x, 1, group).wait_send()
+            y_copy(plane, x, 1, 1 - group).wait_recv()
+
+
+def place_kernel(owners_ref, scales_ref, handed_ref, gathered, placed, scales, rows_out, sems):
+    count, rows, _ = gathered.shape
+    copies = [
+        pltpu.make_async_copy(
+            gathered.at[owners_ref[slot]], placed.at[pl.ds(slot * rows, rows)], sems.at[slot]
+        )
+        for slot in range(count)
+    ]
+    for moving in copies:
+        moving.start()
+    blocks = scales.shape[1] // count
+    lane = lax.broadcasted_iota(jnp.int32, scales_ref.shape[1:], 1)
+    spread = jnp.zeros(scales_ref.shape[1:], jnp.float32)
+    for slot in range(count):
+        spread = jnp.where(lane // blocks == slot, scales_ref[owners_ref[slot]], spread)
+    scales[...] = spread[: scales.shape[0], : scales.shape[1]]
+    tall = handed_ref[...].astype(jnp.float32)
+    row_count = rows_out.shape[0]
+    heads = tall.shape[0] // row_count
+    for row in range(row_count):
+        rows_out[row : row + 1, :] = jnp.concatenate(
+            [tall[row * heads + head : row * heads + head + 1] for head in range(heads)], axis=1
+        ).astype(jnp.bfloat16)
+    for moving in copies:
+        moving.wait()
+
+
+def on_plane(
+    queries,
+    new_keys,
+    new_values,
+    key_cache,
+    value_cache,
+    lengths,
+    base_held,
+    adapter_a,
+    adapter_b,
+    owners,
+):
+    replicas = lax.axis_size("replica")
+    depth = replicas // 2
+    rows, columns = base_held.shape
+    row_count = queries.shape[0]
+    heads = row_count * queries.shape[1] // HD
+    vmem = pl.BlockSpec(memory_space=pltpu.VMEM)
+    smem = pl.BlockSpec(memory_space=pltpu.SMEM)
+    anywhere = pl.BlockSpec(memory_space=pl.ANY)
+    gathered, scales_all, handed = pl.pallas_call(
+        gather_kernel,
+        out_shape=(
+            jax.ShapeDtypeStruct((replicas, rows, columns), jnp.bfloat16),
+            jax.ShapeDtypeStruct((replicas, 8, 128), jnp.float32),
+            jax.ShapeDtypeStruct((heads, HD), jnp.bfloat16),
+        ),
+        in_specs=[vmem, vmem, vmem, smem, vmem, vmem, vmem, anywhere, anywhere],
+        out_specs=(anywhere, anywhere, anywhere),
+        scratch_shapes=[
+            pltpu.VMEM((rows, columns), jnp.bfloat16),
+            pltpu.VMEM((8, 128), jnp.float32),
+            pltpu.VMEM((heads, HD), jnp.bfloat16),
+            pltpu.VMEM(key_cache.shape, jnp.bfloat16),
+            pltpu.VMEM(value_cache.shape, jnp.bfloat16),
+            pltpu.SemaphoreType.DMA((4,)),
+            pltpu.SemaphoreType.DMA((2, depth, 2)),
+            pltpu.SemaphoreType.DMA((depth, 2)),
+            pltpu.SemaphoreType.DMA((depth, 2)),
+            pltpu.SemaphoreType.DMA((depth, 2)),
+            pltpu.SemaphoreType.DMA((2, depth)),
+            pltpu.SemaphoreType.DMA((2, depth)),
+            pltpu.SemaphoreType.DMA((replicas,)),
+            pltpu.SemaphoreType.DMA((replicas,)),
+            pltpu.SemaphoreType.DMA((2,)),
+        ],
+        compiler_params=pltpu.CompilerParams(
+            collective_id=0, has_side_effects=True, vmem_limit_bytes=24 * 2**20
+        ),
+        name="gather",
+    )(
+        queries,
+        new_keys,
+        new_values,
+        lengths,
+        base_held,
+        adapter_a.T,
+        adapter_b,
+        key_cache,
+        value_cache,
+    )
+    block_values, scales, handed_rows = pl.pallas_call(
+        place_kernel,
+        out_shape=(
+            jax.ShapeDtypeStruct((replicas * rows, columns), jnp.bfloat16),
+            jax.ShapeDtypeStruct((columns // BLOCK, replicas * rows // BLOCK), jnp.float32),
+            jax.ShapeDtypeStruct(queries.shape, jnp.bfloat16),
+        ),
+        in_specs=[smem, vmem, vmem, anywhere],
+        out_specs=(anywhere, vmem, vmem),
+        scratch_shapes=[pltpu.SemaphoreType.DMA((replicas,))],
+        name="place",
+    )(owners, scales_all, handed, gathered)
+    return (handed_rows, block_values, scales.T)
+
+
 def solution(mesh):
+    shape = dict(mesh.shape)
+    relay = shape["groups"] == 2 and shape["replica"] % 2 == 0
+
+    def either(*operands):
+        rows, columns = operands[6].shape
+        blocks = shape["replica"] * rows // BLOCK
+        if relay and shape["replica"] <= 16 and rows % BLOCK == 0 and blocks <= 128 and columns <= 8 * BLOCK:
+            return on_plane(*operands)
+        return on_device(*operands)
+
     in_specs = (
         P(("groups", "replica"), "tensor"),
         P(("groups", "replica"), "tensor"),
@@ -102,5 +497,5 @@
     )
     out_specs = (P(("groups", "replica"), "tensor"), P("groups", "tensor"), P("groups", "tensor"))
     return jax.shard_map(
-        on_device, mesh=mesh, in_specs=in_specs, out_specs=out_specs, check_vma=False
-    )
+        either, mesh=mesh, in_specs=in_specs, out_specs=out_specs, check_vma=False
+    )

time: 97.1 us -> 126 us (1.30)
  Pallas kernels: 0 us -> 114 us
  waiting for transfers between devices: 49.7 us -> 0 us
  between operations: 14.1 us -> 0.67 us
  other arithmetic: 10.7 us -> 0 us
  matrix products: 5.6 us -> 0 us
  local copies, waits for them, and re-layouts: 13.5 us -> 10.2 us
  starting transfers between devices: 3.03 us -> 0 us
    pallas_call x0 -> x2, Pallas kernels: none -> 114 us  [the longest x1 82 us: on_plane(): pl.pallas_call(place_kernel, out_shape=(jax.ShapeDtypeStruct((replicas *...]
    all_gather x1 -> x0, waiting for transfers between devices: 45.3 us -> none  [on_device(): everything = lax.all_gather(merged, 'replica', axis=0, tiled=True)]
    gather x2 -> x0, local copies, waits for them, and re-layouts: 8.84 us -> none  [on_device(): jnp.take(everything.reshape(replicas, slice_rows, columns), owners, axis=0)]
    unnamed x9 -> x24, local copies, waits for them, and re-layouts: 1.59 us -> 10.2 us
    dot_general x4 -> x0, matrix products: 5.6 us -> none  [the longest x1 2.1 us: merge_rows(): jnp.dot(factor_rows, adapter_b, preferred_element_type=jnp.float32)]
    reduce_max x1 -> x0, other arithmetic: 5.28 us -> none  [on_device(): block_scales = jnp.max(jnp.abs(tiled), axis=(1, 3)) + 1e-06]
    convert_element_type x2 -> x0, other arithmetic: 4.46 us -> none  [the longest x1 4.45 us: on_device(): (tiled / block_scales[:, None, :, None]).reshape(total_rows, columns)]
    ppermute x1 -> x0, waiting for transfers between devices: 4.39 us -> none  [from_behind(): return lax.ppermute(value, axis, pairs)]
  transfers between devices with their start and end apart: 2 -> 0, of which waited for: 2 -> 0; matrix products, arithmetic and copies ran while one was open for 6% -> 0% of each run, Pallas kernels for 0% -> 0%
where the time goes in v1:
time: 126 us; the launch traced here: 125 us
  Pallas kernels  114 us (90%)
  local copies, waits for them, and re-layouts  10.2 us (8%)
    pallas_call x1, Pallas kernels, on_plane(): pl.pallas_call(place_kernel, out_shape=(jax.ShapeDtypeStruct((replicas *...  82 us
    pallas_call x1, Pallas kernels, on_plane(): pl.pallas_call(gather_kernel, out_shape=(jax.ShapeDtypeStruct((replicas,...  32.2 us
    unnamed x24, local copies, waits for them, and re-layouts  10.2 us

profile of v1, /device:TPU:0, one launch (start us, length us, event | category | flops | bytes accessed | tf_op | source)
XLA Modules:
  0.0 125.1 jit_solution(13837528153457399835)
XLA Ops:
  0.6 0.0 copy-start.1
  0.6 1.2 copy-done.1
  1.9 0.0 copy-start.2
  1.9 1.2 copy-done.2
  3.1 0.0 copy-start.3
  3.1 1.0 copy-done.3
  4.1 0.0 copy-start.5
  4.1 0.7 copy-done.5
  4.8 0.0 copy-start.6
  4.8 0.7 copy-done.6
  5.5 0.0 copy-start.7
  5.5 0.7 copy-done.7
  6.2 0.0 copy-start.9
  6.2 0.7 copy-done.9
  6.9 0.0 copy-start.10
  6.9 0.7 copy-done.10
  7.5 0.0 copy-start.11
  7.5 0.7 copy-done.11
  8.2 32.2 %gather.1 = (bf16[8,640,256]{2,1,0:T(8,128)(2,1)S(1)}, f32[8,8,128]{2,1,0:T(8,128)S(1)}, bf16[32,128]{1,0:T(8,128)(2,1)S(1)}) custom-call(bf16[2,2048]{1,0:T(2,128)(2,1)S(1)} %copy-done.6, bf16[2,256]{1,0:T(2,128)(2,1)S(1)} %copy-done.9, bf16[2,256]{1,0:T(2,128)(2,1)S(1)} %copy-done.10, s32[2]{0:T(128)S(1)} %copy-done.11, bf16[640,256]{1,0:T(8,128)(2,1)S(1)} %copy-done.3, ...), custom_call_target="tpu_custom_call" | custom-call | tf_op jit(solution)/shard_map/gather/pallas_call | solution.py:419
  40.4 0.0 copy-start
  40.4 1.5 %copy-done = bf16[8,640,256]{2,1,0:T(8,128)(2,1)} copy-done((bf16[8,640,256]{2,1,0:T(8,128)(2,1)}, bf16[8,640,256]{2,1,0:T(8,128)(2,1)S(1)}, u32[]{:S(2)}) %copy-start) | copy-done | bytes 2621464
  41.9 0.0 copy-start.4
  41.9 0.6 copy-done.4
  42.5 0.0 copy-start.8
  42.5 0.6 copy-done.8
  43.1 82.0 %place.1 = (bf16[5120,256]{1,0:T(8,128)(2,1)}, f32[2,40]{1,0:T(2,128)}, bf16[2,2048]{1,0:T(2,128)(2,1)}) custom-call(s32[8]{0:T(128)} %owners_ref.1, f32[8,8,128]{2,1,0:T(8,128)} %copy-done.4, bf16[32,128]{1,0:T(8,128)(2,1)} %copy-done.8, bf16[8,640,256]{2,1,0:T(8,128)(2,1)} %copy-done), custom_call_target="tpu_custom_call" | custom-call | tf_op jit(solution)/shard_map/place/pallas_call | solution.py:460
Async XLA Ops:
  0.6 1.2 copy-start.1
  1.9 1.2 copy-start.2
  3.1 1.0 copy-start.3
  4.1 0.7 copy-start.5
  4.8 0.7 copy-start.6
  5.5 0.7 copy-start.7
  6.2 0.7 copy-start.9
  6.9 0.7 copy-start.10
  7.5 0.7 copy-start.11
  40.4 1.5 %copy-start = (bf16[8,640,256]{2,1,0:T(8,128)(2,1)}, bf16[8,640,256]{2,1,0:T(8,128)(2,1)S(1)}, u32[]{:S(2)}) copy-start(bf16[8,640,256]{2,1,0:T(8,128)(2,1)S(1)} %get-tuple-element.11.gathered) | copy-start | bytes 7864324
  41.9 0.6 copy-start.4
  42.5 0.6 copy-start.8

commit v2 on v1

--- a/solution.py
+++ b/solution.py
@@ -148,11 +148,12 @@
     lane = lax.broadcasted_iota(jnp.int32, own_scales.shape, 1)
     line = lax.broadcasted_iota(jnp.int32, own_scales.shape, 0)
     blocks = rows // BLOCK
-    spread = jnp.zeros(own_scales.shape, jnp.float32)
-    for block in range(blocks):
-        part = pl.ds(block * BLOCK, BLOCK)
+
+    def scale_block(step, spread):
+        block = step + group * (blocks - 1 - 2 * step)
+        part = pl.ds(pl.multiple_of(block * BLOCK, BLOCK), BLOCK)
         product = lax.dot_general(
-            factor_ref[:, block * BLOCK : (block + 1) * BLOCK],
+            factor_ref[:, part],
             adapter_b_ref[...],
             (((0,), (0,)), ((), ())),
             preferred_element_type=jnp.float32,
@@ -163,9 +164,7 @@
             scale = jnp.max(jnp.abs(tile), axis=(0, 1), keepdims=True) + 1e-06
             own[part, column * BLOCK : (column + 1) * BLOCK] = (tile / scale).astype(jnp.bfloat16)
             spread = jnp.where((lane % blocks == block) & (line == column), scale, spread)
-    own_scales[...] = spread
-
-    pl.semaphore_wait(barrier, count)
+        return spread
 
     z_end, x_end = sixteen(rows * 31 // 40), sixteen(rows * 3 // 5)
     cut = sixteen(rows * 2 // 5)
@@ -270,7 +269,13 @@
         new_value = new_values_ref[row : row + 1, wide].astype(jnp.float32)
         return mixed + own_weight * new_value
 
-    for piece in range(2):
+    first = -(-cut // BLOCK)
+    spread = jnp.zeros(own_scales.shape, jnp.float32)
+    for piece, steps in enumerate((range(first), range(first, blocks))):
+        for step in steps:
+            spread = scale_block(step, spread)
+        if piece == 0:
+            pl.semaphore_wait(barrier, count)
 
         @pl.when(z < depth - 1)
         def _():
@@ -281,6 +286,7 @@
             z_copy(z, piece, -1, own).start()
 
         x_copy(z, piece, x, own).start()
+    own_scales[...] = spread
     for step in range(1, count):
         scale_copy(step).start()
     own_out = pltpu.make_async_copy(own, gathered.at[me], local_sem.at[2])
@@ -306,10 +312,13 @@
 
     keys_in.wait()
     values_in.wait()
-    units = [(row, head) for row in range(row_count) for head in range(kv_heads)]
-    done = [attend(*unit) for unit in units]
-    tall = jnp.concatenate(done, axis=0)
-    attended[...] = tall.astype(jnp.bfloat16)
+    heads = kv_heads * per_group
+
+    def attend_row(row):
+        tall = jnp.concatenate([attend(row, head) for head in range(kv_heads)], axis=0)
+        attended[row * heads : (row + 1) * heads, :] = tall.astype(jnp.bfloat16)
+
+    attend_row(0)
     hand = pltpu.make_async_remote_copy(
         src_ref=attended,
         dst_ref=handed,
@@ -317,9 +326,11 @@
         recv_sem=hand_sem.at[1],
         device_id={"replica": lax.rem(me + 1, count)},
     )
-    hand.start()
-
     for step in range(1, depth + 1):
+        if step == 2:
+            for row in range(1, row_count):
+                attend_row(row)
+            hand.start()
         for piece in range(2):
             if step < depth:
 
@@ -369,15 +380,24 @@
             y_copy(plane, x, 1, 1 - group).wait_recv()
 
 
-def place_kernel(owners_ref, scales_ref, handed_ref, gathered, placed, scales, rows_out, sems):
+def place_kernel(
+    owners_ref, scales_ref, handed_ref, gathered, placed, scales, rows_out, held, in_sems, out_sems
+):
     count, rows, _ = gathered.shape
+    fetches = [
+        pltpu.make_async_copy(gathered.at[owners_ref[slot]], held.at[slot], in_sems.at[slot])
+        for slot in range(count)
+    ]
     copies = [
         pltpu.make_async_copy(
-            gathered.at[owners_ref[slot]], placed.at[pl.ds(slot * rows, rows)], sems.at[slot]
+            held.at[slot], placed.at[pl.ds(slot * rows, rows)], out_sems.at[slot]
         )
         for slot in range(count)
     ]
-    for moving in copies:
+    for moving in fetches:
+        moving.start()
+    for fetch, moving in zip(fetches, copies):
+        fetch.wait()
         moving.start()
     blocks = scales.shape[1] // count
     lane = lax.broadcasted_iota(jnp.int32, scales_ref.shape[1:], 1)
@@ -443,7 +463,7 @@
             pltpu.SemaphoreType.DMA((2,)),
         ],
         compiler_params=pltpu.CompilerParams(
-            collective_id=0, has_side_effects=True, vmem_limit_bytes=24 * 2**20
+            collective_id=0, has_side_effects=True, vmem_limit_bytes=60 * 2**20
         ),
         name="gather",
     )(
@@ -466,7 +486,12 @@
         ),
         in_specs=[smem, vmem, vmem, anywhere],
         out_specs=(anywhere, vmem, vmem),
-        scratch_shapes=[pltpu.SemaphoreType.DMA((replicas,))],
+        scratch_shapes=[
+            pltpu.VMEM((replicas, rows, columns), jnp.bfloat16),
+            pltpu.SemaphoreType.DMA((replicas,)),
+            pltpu.SemaphoreType.DMA((replicas,)),
+        ],
+        compiler_params=pltpu.CompilerParams(vmem_limit_bytes=60 * 2**20),
         name="place",
     )(owners, scales_all, handed, gathered)
     return (handed_rows, block_values, scales.T)

time: 126 us -> 38.1 us (0.30)
  Pallas kernels: 114 us -> 37.2 us
  local copies, waits for them, and re-layouts: 10.2 us -> 0 us
    pallas_call x1, Pallas kernels: 82 us -> 3.97 us  [on_plane(): pl.pallas_call(place_kernel, out_shape=(jax.ShapeDtypeStruct((replicas *...]
    unnamed x24 -> x0, local copies, waits for them, and re-layouts: 10.2 us -> none
where the time goes in v2:
time: 38.1 us; the launch traced here: 37.8 us
  Pallas kernels  37.2 us (98%)
  between operations  0.64 us (2%)
    pallas_call x1, Pallas kernels, on_plane(): pl.pallas_call(gather_kernel, out_shape=(jax.ShapeDtypeStruct((replicas,...  33.2 us
    pallas_call x1, Pallas kernels, on_plane(): pl.pallas_call(place_kernel, out_shape=(jax.ShapeDtypeStruct((replicas *...  3.97 us

profile of v2, /device:TPU:0, one launch (start us, length us, event | category | flops | bytes accessed | tf_op | source)
XLA Modules:
  0.0 37.8 jit_solution(8204027999316878718)
XLA Ops:
  0.6 33.2 %gather.1 = (bf16[8,640,256]{2,1,0:T(8,128)(2,1)}, f32[8,8,128]{2,1,0:T(8,128)}, bf16[32,128]{1,0:T(8,128)(2,1)}) custom-call(bf16[2,2048]{1,0:T(2,128)(2,1)} %queries_ref.1, bf16[2,256]{1,0:T(2,128)(2,1)} %new_keys_ref.1, bf16[2,256]{1,0:T(2,128)(2,1)} %new_values_ref.1, s32[2]{0:T(128)} %lengths_ref.1, bf16[640,256]{1,0:T(8,128)(2,1)} %base_ref.1, ...), custom_call_target="tpu_custom_call" | custom-call | tf_op jit(solution)/shard_map/gather/pallas_call | solution.py:439
  33.9 4.0 %place.1 = (bf16[5120,256]{1,0:T(8,128)(2,1)}, f32[2,40]{1,0:T(2,128)}, bf16[2,2048]{1,0:T(2,128)(2,1)}) custom-call(s32[8]{0:T(128)} %owners_ref.1, f32[8,8,128]{2,1,0:T(8,128)} %get-tuple-element.9.scales_ref, bf16[32,128]{1,0:T(8,128)(2,1)} %get-tuple-element.10.handed_ref, bf16[8,640,256]{2,1,0:T(8,128)(2,1)} %get-tuple-element.11.gathered), custom_call_target="tpu_custom_call" | custom-call | tf_op jit(solution)/shard_map/place/pallas_call | solution.py:480

commit v3 on v2

--- a/solution.py
+++ b/solution.py
@@ -89,18 +89,14 @@
     return (handed_rows, block_values, block_scales)
 
 
-def sixteen(rows):
-    return max(16, rows // 16 * 16)
-
-
 def gather_kernel(
-    queries_ref,
-    new_keys_ref,
-    new_values_ref,
-    lengths_ref,
-    base_ref,
-    factor_ref,
-    adapter_b_ref,
+    queries_hbm,
+    new_keys_hbm,
+    new_values_hbm,
+    lengths_hbm,
+    base_hbm,
+    factor_hbm,
+    adapter_b_hbm,
     keys_hbm,
     values_hbm,
     gathered,
@@ -111,6 +107,13 @@
     attended,
     keys,
     values,
+    queries_ref,
+    new_keys_ref,
+    new_values_ref,
+    lengths_ref,
+    base_ref,
+    factor_ref,
+    adapter_b_ref,
     local_sem,
     z_send,
     z_recv,
@@ -133,11 +136,6 @@
     kv_heads = columns // HD
     per_group = queries_ref.shape[1] // HD // kv_heads
 
-    keys_in = pltpu.make_async_copy(keys_hbm, keys, local_sem.at[0])
-    values_in = pltpu.make_async_copy(values_hbm, values, local_sem.at[1])
-    keys_in.start()
-    values_in.start()
-
     barrier = pltpu.get_barrier_semaphore()
     for step in range(1, count):
         pl.semaphore_signal(
@@ -145,6 +143,25 @@
         )
     pl.semaphore_signal(barrier, inc=1, device_id={"groups": 1 - group})
 
+    places = (
+        (base_hbm, base_ref),
+        (factor_hbm, factor_ref),
+        (adapter_b_hbm, adapter_b_ref),
+        (keys_hbm, keys),
+        (values_hbm, values),
+        (queries_hbm, queries_ref),
+        (new_keys_hbm, new_keys_ref),
+        (new_values_hbm, new_values_ref),
+        (lengths_hbm, lengths_ref),
+    )
+    arriving = [
+        pltpu.make_async_copy(source, target, local_sem.at[2 + number])
+        for number, (source, target) in enumerate(places)
+    ]
+    for moving in arriving:
+        moving.start()
+    for moving in arriving[:3]:
+        moving.wait()
     lane = lax.broadcasted_iota(jnp.int32, own_scales.shape, 1)
     line = lax.broadcasted_iota(jnp.int32, own_scales.shape, 0)
     blocks = rows // BLOCK
@@ -166,16 +183,13 @@
             spread = jnp.where((lane % blocks == block) & (line == column), scale, spread)
         return spread
 
-    z_end, x_end = sixteen(rows * 31 // 40), sixteen(rows * 3 // 5)
-    cut = sixteen(rows * 2 // 5)
-    z_pieces = ((0, cut), (cut, z_end))
-    x_pieces = ((0, cut), (cut, x_end))
-    yx_piece, yz_piece = (0, rows - x_end), (0, rows - z_end)
+    z_pieces = blocks - 1
+    x_pieces = max(blocks - blocks // 2, 1)
+    yx_pieces, yz_pieces = blocks - x_pieces, 1
 
     def window(ref, piece, side):
-        low, high = piece
-        start = pl.multiple_of(low + side * (rows - high - low), 16)
-        return ref.at[pl.ds(start, high - low)]
+        block = piece + side * (blocks - 1 - 2 * piece)
+        return ref.at[pl.ds(pl.multiple_of(block * BLOCK, BLOCK), BLOCK)]
 
     def copy(source, plane, column, piece, side, send, recv, device):
         target = gathered.at[plane * 2 + column]
@@ -193,7 +207,7 @@
             source,
             plane,
             x,
-            z_pieces[piece],
+            piece,
             group,
             z_send.at[(way + 1) // 2, plane, piece],
             z_recv.at[plane, piece],
@@ -205,22 +219,23 @@
             source,
             plane,
             column,
-            x_pieces[piece],
+            piece,
             group,
             x_send.at[plane, piece],
             x_recv.at[plane, piece],
             {"replica": z * 2 + 1 - x},
         )
 
-    def y_copy(plane, column, which, side):
+    def y_copy(plane, column, piece, side):
+        slot = jnp.where(column == x, x_pieces, 0) + piece
         return copy(
             None,
             plane,
             column,
-            (yx_piece, yz_piece)[which],
+            piece,
             side,
-            y_send.at[which, plane],
-            y_recv.at[which, plane],
+            y_send.at[plane, slot],
+            y_recv.at[plane, slot],
             {"groups": 1 - group},
         )
 
@@ -269,29 +284,29 @@
         new_value = new_values_ref[row : row + 1, wide].astype(jnp.float32)
         return mixed + own_weight * new_value
 
-    first = -(-cut // BLOCK)
     spread = jnp.zeros(own_scales.shape, jnp.float32)
-    for piece, steps in enumerate((range(first), range(first, blocks))):
-        for step in steps:
-            spread = scale_block(step, spread)
+    for piece in range(blocks):
+        spread = scale_block(piece, spread)
         if piece == 0:
             pl.semaphore_wait(barrier, count)
-
-        @pl.when(z < depth - 1)
-        def _():
-            z_copy(z, piece, 1, own).start()
-
-        @pl.when(z > 0)
-        def _():
-            z_copy(z, piece, -1, own).start()
-
-        x_copy(z, piece, x, own).start()
+        if piece < z_pieces:
+
+            @pl.when(z < depth - 1)
+            def _():
+                z_copy(z, piece, 1, own).start()
+
+            @pl.when(z > 0)
+            def _():
+                z_copy(z, piece, -1, own).start()
+
+        if piece < x_pieces:
+            x_copy(z, piece, x, own).start()
     own_scales[...] = spread
     for step in range(1, count):
         scale_copy(step).start()
-    own_out = pltpu.make_async_copy(own, gathered.at[me], local_sem.at[2])
+    own_out = pltpu.make_async_copy(own, gathered.at[me], local_sem.at[0])
     own_out.start()
-    scales_out = pltpu.make_async_copy(own_scales, scales_all.at[me], local_sem.at[3])
+    scales_out = pltpu.make_async_copy(own_scales, scales_all.at[me], local_sem.at[1])
     scales_out.start()
 
     def z_step(plane, piece, way):
@@ -301,17 +316,18 @@
         def _():
             z_copy(plane, piece, way).start()
 
-        x_copy(plane, piece, x).start()
-        if piece == 0:
-            y_copy(plane, x, 1, group).start()
+        if piece < x_pieces:
+            x_copy(plane, piece, x).start()
+        if piece < yz_pieces:
+            y_copy(plane, x, piece, group).start()
 
     def x_step(plane, piece):
         x_copy(plane, piece, 1 - x).wait_recv()
-        if piece == 0:
-            y_copy(plane, 1 - x, 0, group).start()
-
-    keys_in.wait()
-    values_in.wait()
+        if piece < yx_pieces:
+            y_copy(plane, 1 - x, piece, group).start()
+
+    for moving in arriving[3:]:
+        moving.wait()
     heads = kv_heads * per_group
 
     def attend_row(row):
@@ -331,7 +347,7 @@
             for row in range(1, row_count):
                 attend_row(row)
             hand.start()
-        for piece in range(2):
+        for piece in range(z_pieces):
             if step < depth:
 
                 @pl.when(z - step >= 0)
@@ -342,17 +358,18 @@
                 def _():
                     z_step(z + step, piece, -1)
 
-            if step == 1:
-                x_step(z, piece)
-            else:
-
-                @pl.when(z - step + 1 >= 0)
-                def _():
-                    x_step(z - step + 1, piece)
-
-                @pl.when(z + step - 1 < depth)
-                def _():
-                    x_step(z + step - 1, piece)
+            if piece < x_pieces:
+                if step == 1:
+                    x_step(z, piece)
+                else:
+
+                    @pl.when(z - step + 1 >= 0)
+                    def _():
+                        x_step(z - step + 1, piece)
+
+                    @pl.when(z + step - 1 < depth)
+                    def _():
+                        x_step(z + step - 1, piece)
 
     own_out.wait()
     scales_out.wait()
@@ -360,7 +377,7 @@
     for step in range(1, count):
         scale_copy(step).wait()
     for plane in range(depth):
-        for piece in range(2):
+        for piece in range(z_pieces):
 
             @pl.when((plane <= z) & (z < depth - 1))
             def _():
@@ -370,14 +387,17 @@
             def _():
                 z_copy(plane, piece, -1).wait_send()
 
+        for piece in range(x_pieces):
             x_copy(plane, piece, x).wait_send()
-        y_copy(plane, 1 - x, 0, group).wait_send()
-        y_copy(plane, 1 - x, 0, 1 - group).wait_recv()
+        for piece in range(yx_pieces):
+            y_copy(plane, 1 - x, piece, group).wait_send()
+            y_copy(plane, 1 - x, piece, 1 - group).wait_recv()
 
         @pl.when(z != plane)
         def _():
-            y_copy(plane, x, 1, group).wait_send()
-            y_copy(plane, x, 1, 1 - group).wait_recv()
+            for piece in range(yz_pieces):
+                y_copy(plane, x, piece, group).wait_send()
+                y_copy(plane, x, piece, 1 - group).wait_recv()
 
 
 def place_kernel(
@@ -431,11 +451,13 @@
     replicas = lax.axis_size("replica")
     depth = replicas // 2
     rows, columns = base_held.shape
+    blocks = rows // BLOCK
     row_count = queries.shape[0]
     heads = row_count * queries.shape[1] // HD
     vmem = pl.BlockSpec(memory_space=pltpu.VMEM)
     smem = pl.BlockSpec(memory_space=pltpu.SMEM)
     anywhere = pl.BlockSpec(memory_space=pl.ANY)
+    hbm = pl.BlockSpec(memory_space=pltpu.HBM)
     gathered, scales_all, handed = pl.pallas_call(
         gather_kernel,
         out_shape=(
@@ -443,7 +465,7 @@
             jax.ShapeDtypeStruct((replicas, 8, 128), jnp.float32),
             jax.ShapeDtypeStruct((heads, HD), jnp.bfloat16),
         ),
-        in_specs=[vmem, vmem, vmem, smem, vmem, vmem, vmem, anywhere, anywhere],
+        in_specs=[hbm, hbm, hbm, hbm, hbm, hbm, hbm, hbm, hbm],
         out_specs=(anywhere, anywhere, anywhere),
         scratch_shapes=[
             pltpu.VMEM((rows, columns), jnp.bfloat16),
@@ -451,13 +473,20 @@
             pltpu.VMEM((heads, HD), jnp.bfloat16),
             pltpu.VMEM(key_cache.shape, jnp.bfloat16),
             pltpu.VMEM(value_cache.shape, jnp.bfloat16),
-            pltpu.SemaphoreType.DMA((4,)),
-            pltpu.SemaphoreType.DMA((2, depth, 2)),
-            pltpu.SemaphoreType.DMA((depth, 2)),
-            pltpu.SemaphoreType.DMA((depth, 2)),
-            pltpu.SemaphoreType.DMA((depth, 2)),
-            pltpu.SemaphoreType.DMA((2, depth)),
-            pltpu.SemaphoreType.DMA((2, depth)),
+            pltpu.VMEM(queries.shape, jnp.bfloat16),
+            pltpu.VMEM(new_keys.shape, jnp.bfloat16),
+            pltpu.VMEM(new_values.shape, jnp.bfloat16),
+            pltpu.SMEM(lengths.shape, jnp.int32),
+            pltpu.VMEM(base_held.shape, jnp.bfloat16),
+            pltpu.VMEM(adapter_a.shape[::-1], jnp.bfloat16),
+            pltpu.VMEM(adapter_b.shape, jnp.bfloat16),
+            pltpu.SemaphoreType.DMA((11,)),
+            pltpu.SemaphoreType.DMA((2, depth, blocks)),
+            pltpu.SemaphoreType.DMA((depth, blocks)),
+            pltpu.SemaphoreType.DMA((depth, blocks)),
+            pltpu.SemaphoreType.DMA((depth, blocks)),
+            pltpu.SemaphoreType.DMA((depth, blocks)),
+            pltpu.SemaphoreType.DMA((depth, blocks)),
             pltpu.SemaphoreType.DMA((replicas,)),
             pltpu.SemaphoreType.DMA((replicas,)),
             pltpu.SemaphoreType.DMA((2,)),
@@ -504,7 +533,7 @@
     def either(*operands):
         rows, columns = operands[6].shape
         blocks = shape["replica"] * rows // BLOCK
-        if relay and shape["replica"] <= 16 and rows % BLOCK == 0 and blocks <= 128 and columns <= 8 * BLOCK:
+        if relay and shape["replica"] <= 16 and rows % BLOCK == 0 and rows > 2 * BLOCK and blocks <= 128 and columns <= 8 * BLOCK:
             return on_plane(*operands)
         return on_device(*operands)
 

time: 38.1 us -> 36.6 us (0.961)
  Pallas kernels: 37.2 us -> 35.7 us
    pallas_call x1, Pallas kernels: 33.2 us -> 31.7 us  [on_plane(): pl.pallas_call(gather_kernel, out_shape=(jax.ShapeDtypeStruct((replicas,...]
where the time goes in v3:
time: 36.6 us; the launch traced here: 36.3 us
  Pallas kernels  35.7 us (98%)
  between operations  0.64 us (2%)
    pallas_call x1, Pallas kernels, on_plane(): pl.pallas_call(gather_kernel, out_shape=(jax.ShapeDtypeStruct((replicas,...  31.7 us
    pallas_call x1, Pallas kernels, on_plane(): pl.pallas_call(place_kernel, out_shape=(jax.ShapeDtypeStruct((replicas *...  3.97 us

profile of v3, /device:TPU:0, one launch (start us, length us, event | category | flops | bytes accessed | tf_op | source)
XLA Modules:
  0.0 36.3 jit_solution(911381795603689783)
XLA Ops:
  0.6 31.7 %gather.1 = (bf16[8,640,256]{2,1,0:T(8,128)(2,1)}, f32[8,8,128]{2,1,0:T(8,128)}, bf16[32,128]{1,0:T(8,128)(2,1)}) custom-call(bf16[2,2048]{1,0:T(2,128)(2,1)} %queries_hbm.1, bf16[2,256]{1,0:T(2,128)(2,1)} %new_keys_hbm.1, bf16[2,256]{1,0:T(2,128)(2,1)} %new_values_hbm.1, s32[2]{0:T(128)} %lengths_hbm.1, bf16[640,256]{1,0:T(8,128)(2,1)} %base_hbm.1, ...), custom_call_target="tpu_custom_call" | custom-call | tf_op jit(solution)/shard_map/gather/pallas_call | solution.py:461
  32.4 4.0 %place.1 = (bf16[5120,256]{1,0:T(8,128)(2,1)}, f32[2,40]{1,0:T(2,128)}, bf16[2,2048]{1,0:T(2,128)(2,1)}) custom-call(s32[8]{0:T(128)} %owners_ref.1, f32[8,8,128]{2,1,0:T(8,128)} %get-tuple-element.9.scales_ref, bf16[32,128]{1,0:T(8,128)(2,1)} %get-tuple-element.10.handed_ref, bf16[8,640,256]{2,1,0:T(8,128)(2,1)} %get-tuple-element.11.gathered), custom_call_target="tpu_custom_call" | custom-call | tf_op jit(solution)/shard_map/place/pallas_call | solution.py:509
